TPU v7x, 128 devices: a whole 4x4x4 slice. The times are simulated.
128 devices in a mesh: inp: 8 (over y, z_hi), tm: 16 (over x, z_lo, core).
Axes of the slice: x: 4, y: 4, z: 4 (z_hi: 2, z_lo: 2; z = z_hi * 2 + z_lo), core: 2. Of those that a mesh axis runs over, the one named last changes fastest.
Arguments:
- volt: bfloat16 [512, 573440], P('inp', 'tm'), may hold values from -800 to 800
Outputs:
- visibility: float32 [512, 2, 512, 512], P(('inp', 'tm'))
All inputs are finite; a program needn't handle non-finite values.
Results may differ from a plain program's by a relative error of at most 0.0013.
Values may be sent and summed in bfloat16 or wider, within the bound.
A program may use at most 128 MiB of HBM per device.

v0:
```python
import functools
import itertools

import jax
import jax.numpy as jnp
import ml_dtypes
import numpy as np
from jax import lax
from jax.experimental import pallas as pl
from jax.experimental.pallas import tpu as pltpu
from jax.sharding import PartitionSpec as P

MESH = pl.DeviceIdType.MESH
FRAME = 1024
TAPS = 4
INPUTS = 64
FRAMES = 32
PAIRS = 16
CHIPS = 64
UNIT = 16
CHUNK = 16
ROWS = CHUNK * UNIT
PITCH = ROWS + 8
TOTAL = 512
LIFT = 2.0**32


def window_table():
    index = np.arange(TAPS * FRAME, dtype=np.float64)
    shifted = (index - TAPS * FRAME / 2 + 0.5) / FRAME
    shaped = np.sinc(shifted) * (0.54 - 0.46 * np.cos(2.0 * np.pi * index / (TAPS * FRAME - 1)))
    return (shaped.reshape(TAPS, FRAME) * LIFT).astype(np.float32)


def twiddle_table():
    chans = FRAME // 2
    turn = np.arange(chans)[:, None] * np.arange(FRAME)[None, :] % FRAME
    phase = turn.astype(np.float32) * np.float32(2.0 * np.pi / FRAME)
    phase = phase.astype(np.float64)
    pair = np.stack([np.cos(phase), -np.sin(phase)], axis=1)
    return pair.reshape(2 * chans, FRAME).astype(np.float32).astype(ml_dtypes.bfloat16)


def chip_order():
    offsets = list(itertools.product(range(4), repeat=3))[1:]
    orbits, seen = [], set()
    for start in offsets:
        if start in seen:
            continue
        orbit, now = [], start
        for _ in range(3):
            for one in (now, tuple((4 - v) % 4 for v in now)):
                if one not in orbit:
                    orbit.append(one)
            now = (now[1], now[2], now[0])
        seen.update(orbit)
        orbits.append(orbit)
    mixed = np.random.RandomState(1).permutation(len(orbits))
    return [o for i in mixed for o in orbits[i]] + [(0, 0, 0)]


ORDER = chip_order()


def channelize(volt, window, table, out, raw, filtered, rows, spectra, sendbuf, raw_sem, row_sem, send_sem, recv_sem, own_sem):
    row, column = lax.axis_index("inp"), lax.axis_index("tm")
    x, y, z, core = column // 4, row // 2, (row % 2) * 2 + (column // 2) % 2, column % 2
    me = row * 16 + column

    barrier = pltpu.get_barrier_semaphore()

    def greet(step, carry):
        other = lax.rem(me + step, 128)
        pl.semaphore_signal(barrier, inc=1, device_id=(other // 16, other % 16), device_id_type=MESH)
        return carry

    tiles = INPUTS // 16
    loads = [
        pltpu.make_async_copy(volt.at[pl.ds(16 * i, 16)], raw.at[pl.ds(16 * i, 16)], raw_sem.at[i])
        for i in range(tiles)
    ]
    for load in loads:
        load.start()
    lax.fori_loop(1, 128, greet, 0)

    places = []
    for k, (dx, dy, dz) in enumerate(ORDER):
        px, py, pz = lax.rem(x + dx, 4), lax.rem(y + dy, 4), lax.rem(z + dz, 4)
        inp, tm = py * 2 + pz // 2, px * 4 + lax.rem(pz, 2) * 2
        places.append((inp, tm))
        chip = inp * 8 + tm // 2
        source = table.at[pl.ds(pl.multiple_of(chip * UNIT, UNIT), UNIT)]
        pltpu.make_async_copy(source, rows.at[pl.ds(k * UNIT, UNIT)], row_sem.at[k // CHUNK]).start()

    for i in range(tiles):
        loads[i].wait()

        def filter_tile(j, carry, i=i):
            at = pl.multiple_of(j * 128, 128)
            taps = [window[pl.ds(k, 1), pl.ds(at, 128)] for k in range(TAPS)]
            held = []
            for f in range(FRAMES + TAPS - 1):
                held.append(raw[pl.ds(16 * i, 16), pl.ds(f * FRAME + at, 128)].astype(jnp.float32))
                if f >= TAPS - 1:
                    total = taps[0] * held[0]
                    for k in range(1, TAPS):
                        total = total + taps[k] * held[k]
                    held.pop(0)
                    g = f - TAPS + 1
                    filtered[pl.ds(g * INPUTS + 16 * i, 16), pl.ds(at, 128)] = total.astype(jnp.bfloat16)
            return carry

        lax.fori_loop(0, FRAME // 128, filter_tile, 0)

    copies = []
    for chunk in range(CHIPS // CHUNK):
        here = rows.at[pl.ds(chunk * ROWS, ROWS)]
        pltpu.make_async_copy(table.at[pl.ds(0, ROWS)], here, row_sem.at[chunk]).wait()

        def transform(n, carry, here=here):
            block = filtered[pl.ds(pl.multiple_of(n * 256, 256), 256), :]
            product = lax.dot_general(
                here[...], block, (((1,), (1,)), ((), ())), preferred_element_type=jnp.float32
            )
            for h in range(2):
                at = pl.multiple_of((2 * n + h) * PITCH, 8)
                spectra[pl.ds(at, ROWS), :] = product[:, h * 128 : (h + 1) * 128]
            return carry

        lax.fori_loop(0, PAIRS // 2, transform, 0)

        def gather(u, carry, chunk=chunk):
            for r in range(UNIT):
                part = spectra[pl.ds(u * UNIT + r, PAIRS, stride=PITCH), :]
                sendbuf[chunk * CHUNK + u, r] = part.astype(jnp.bfloat16)
            return carry

        lax.fori_loop(0, CHUNK, gather, 0)

        if chunk == 0:
            pl.semaphore_wait(barrier, 127)
        for k in range(chunk * CHUNK, (chunk + 1) * CHUNK):
            inp, tm = places[k]
            for turn in range(2):
                to = lax.rem(core + turn, 2)
                half = sendbuf.at[k, pl.ds(to * 8, 8)]
                if ORDER[k] == (0, 0, 0) and turn == 0:
                    copy = pltpu.make_async_copy(half, out.at[me], own_sem)
                else:
                    copy = pltpu.make_async_remote_copy(
                        src_ref=half,
                        dst_ref=out.at[me],
                        send_sem=send_sem.at[k, turn],
                        recv_sem=recv_sem.at[k, turn],
                        device_id=(inp, tm + to),
                        device_id_type=MESH,
                    )
                copy.start()
                copies.append(copy)
    for copy in copies:
        copy.wait()


def correlate(block, out, parts):
    lane = lax.broadcasted_iota(jnp.int32, (256, 128), 1)
    for p in range(2):
        for k in range(4):
            even = block[32 * k : 32 * k + 16, 0, p].reshape(256, 128)
            odd = block[32 * k + 16 : 32 * k + 32, 0, p].reshape(256, 128)
            first = jnp.concatenate([even[:, :64], odd[:, :64]], axis=1)
            second = jnp.concatenate([even[:, 64:], odd[:, 64:]], axis=1)
            parts[512 * p : 512 * p + 256, 128 * k : 128 * k + 128] = first
            parts[512 * p + 256 : 512 * p + 512, 128 * k : 128 * k + 128] = second
    dims = (((0,), (0,)), ((), ()))
    both = parts[...]
    real = lax.dot_general(both, both, dims, preferred_element_type=jnp.float32)
    cross = lax.dot_general(parts[512:, :], parts[:512, :], dims, preferred_element_type=jnp.float32)
    imag = cross - cross.T
    same = lax.broadcasted_iota(jnp.int32, (128, 128), 0) == lax.broadcasted_iota(jnp.int32, (128, 128), 1)
    along, down = [], []
    for k in range(4):
        tile = jnp.where(same, real[128 * k : 128 * k + 128, 128 * k : 128 * k + 128], 0.0)
        along.append(jnp.sum(tile, axis=0, keepdims=True))
        down.append(jnp.sum(tile, axis=1, keepdims=True))

    def scale(power):
        return lax.rsqrt(power * (LIFT**-2 / TOTAL) + 1e-06) * (1.0 / LIFT)

    along = scale(jnp.concatenate(along, axis=1)) * (1.0 / TOTAL)
    down = scale(jnp.concatenate(down, axis=0))
    out[0, 0] = real * along * down
    out[0, 1] = imag * along * down


def on_device(volt):
    block = pl.pallas_call(
        channelize,
        out_shape=jax.ShapeDtypeStruct((128, 8, PAIRS, 128), jnp.bfloat16),
        in_specs=[
            pl.BlockSpec(memory_space=pl.ANY),
            pl.BlockSpec(memory_space=pltpu.VMEM),
            pl.BlockSpec(memory_space=pl.ANY),
        ],
        out_specs=pl.BlockSpec(memory_space=pl.ANY),
        scratch_shapes=[
            pltpu.VMEM((INPUTS, (FRAMES + TAPS - 1) * FRAME), jnp.bfloat16),
            pltpu.VMEM((FRAMES * INPUTS, FRAME), jnp.bfloat16),
            pltpu.VMEM((CHIPS * UNIT, FRAME), jnp.bfloat16),
            pltpu.VMEM((PAIRS * PITCH, 128), jnp.float32),
            pltpu.VMEM((CHIPS, UNIT, PAIRS, 128), jnp.bfloat16),
            pltpu.SemaphoreType.DMA((INPUTS // 16,)),
            pltpu.SemaphoreType.DMA((CHIPS // CHUNK,)),
            pltpu.SemaphoreType.DMA((CHIPS, 2)),
            pltpu.SemaphoreType.DMA((CHIPS, 2)),
            pltpu.SemaphoreType.DMA,
        ],
        compiler_params=pltpu.CompilerParams(
            collective_id=0, has_side_effects=True, vmem_limit_bytes=48 << 20
        ),
        name="channelize",
    )(volt, jnp.asarray(window_table()), jnp.asarray(twiddle_table()))
    block = block.reshape(128, 4, 2, PAIRS, 128)
    return pl.pallas_call(
        correlate,
        grid=(4,),
        out_shape=jax.ShapeDtypeStruct((4, 2, 512, 512), jnp.float32),
        in_specs=[pl.BlockSpec((128, 1, 2, PAIRS, 128), lambda c: (0, c, 0, 0, 0))],
        out_specs=pl.BlockSpec((1, 2, 512, 512), lambda c: (c, 0, 0, 0)),
        scratch_shapes=[pltpu.VMEM((1024, 512), jnp.bfloat16)],
        compiler_params=pltpu.CompilerParams(vmem_limit_bytes=48 << 20),
        name="correlate",
    )(block)


def solution(mesh):
    return jax.shard_map(
        on_device,
        mesh=mesh,
        in_specs=(P("inp", "tm"),),
        out_specs=P(("inp", "tm"), None, None, None),
        check_vma=False,
    )
```

profile of v0, /device:TPU:1, one launch (start us, length us, event | category | flops | bytes accessed | tf_op | source)
XLA Modules:
  0.0 82.8 jit_solution(15048629937431722517)
XLA Ops:
  0.0 0.0 copy-start.1
  0.0 1.6 %copy-done.1 = bf16[1024,1024]{1,0:T(8,128)(2,1)S(1)} copy-done((bf16[1024,1024]{1,0:T(8,128)(2,1)S(1)}, bf16[1024,1024]{1,0:T(8,128)(2,1)}, u32[]{:S(2)}) %copy-start.1) | copy-done | bytes 2097176
  1.6 0.0 copy-start.2
  1.6 0.7 copy-done.2
  2.3 69.0 %channelize.1 = bf16[128,8,16,128]{3,2,1,0:T(8,128)(2,1)} custom-call(bf16[64,35840]{1,0:T(8,128)(2,1)} %volt.1, f32[4,1024]{1,0:T(4,128)S(1)} %copy-done.2, bf16[1024,1024]{1,0:T(8,128)(2,1)S(1)} %copy-done.1), custom_call_target="tpu_custom_call" | custom-call | tf_op jit(solution)/shard_map/channelize/pallas_call | solution.py:196
  71.3 0.0 copy-start
  71.3 2.2 %copy-done = bf16[128,8,16,128]{3,2,1,0:T(8,128)(2,1)S(1)} copy-done((bf16[128,8,16,128]{3,2,1,0:T(8,128)(2,1)S(1)}, bf16[128,8,16,128]{3,2,1,0:T(8,128)(2,1)}, u32[]{:S(2)}) %copy-start) | copy-done | bytes 4194328
  73.5 9.3 %correlate.1 = f32[4,2,512,512]{3,2,1,0:T(8,128)} custom-call(bf16[128,4,2,16,128]{4,3,2,1,0:T(8,128)(2,1)S(1)} %bitcast.1), custom_call_target="tpu_custom_call" | custom-call | tf_op jit(solution)/shard_map/correlate/pallas_call | solution.py:223
Async XLA Ops:
  0.0 1.6 %copy-start.1 = (bf16[1024,1024]{1,0:T(8,128)(2,1)S(1)}, bf16[1024,1024]{1,0:T(8,128)(2,1)}, u32[]{:S(2)}) copy-start(bf16[1024,1024]{1,0:T(8,128)(2,1)} %constant.5.clone.table) | copy-start | bytes 6291460
  1.6 0.7 copy-start.2
  71.3 2.2 %copy-start = (bf16[128,8,16,128]{3,2,1,0:T(8,128)(2,1)S(1)}, bf16[128,8,16,128]{3,2,1,0:T(8,128)(2,1)}, u32[]{:S(2)}) copy-start(bf16[128,8,16,128]{3,2,1,0:T(8,128)(2,1)} %channelize.1) | copy-start | bytes 12582916
where the time goes:
time: 83.1 us; the launch traced here: 82.8 us
  Pallas kernels  78.3 us (94%)
  local copies, waits for them, and re-layouts  4.49 us (5%)
    pallas_call x1, Pallas kernels, on_device(): pl.pallas_call(channelize, out_shape=jax.ShapeDtypeStruct((128, 8, PAIRS,...  69 us
    pallas_call x1, Pallas kernels, on_device(): pl.pallas_call(correlate, grid=(4,), out_shape=jax.ShapeDtypeStruct((4, 2...  9.35 us
    unnamed x6, local copies, waits for them, and re-layouts  4.49 us

commit v1 on v0

v1 whole, which is shorter than its diff:
```python
import functools
import itertools

import jax
import jax.numpy as jnp
import ml_dtypes
import numpy as np
from jax import lax
from jax.experimental import pallas as pl
from jax.experimental.pallas import tpu as pltpu
from jax.sharding import PartitionSpec as P

MESH = pl.DeviceIdType.MESH
FRAME = 1024
TAPS = 4
INPUTS = 64
FRAMES = 32
HALF = 16
PAIRS = 8
CHIPS = 64
UNIT = 16
CHUNK = 16
ROWS = CHUNK * UNIT
PITCH = ROWS + 8
TOTAL = 512
LIFT = 2.0**32


def window_table():
    index = np.arange(TAPS * FRAME, dtype=np.float64)
    shifted = (index - TAPS * FRAME / 2 + 0.5) / FRAME
    shaped = np.sinc(shifted) * (0.54 - 0.46 * np.cos(2.0 * np.pi * index / (TAPS * FRAME - 1)))
    return (shaped.reshape(TAPS, FRAME) * LIFT).astype(np.float32)


def twiddle_table():
    chans = FRAME // 2
    turn = np.arange(chans)[:, None] * np.arange(FRAME)[None, :] % FRAME
    phase = turn.astype(np.float32) * np.float32(2.0 * np.pi / FRAME)
    phase = phase.astype(np.float64)
    pair = np.stack([np.cos(phase), -np.sin(phase)], axis=1)
    return pair.reshape(2 * chans, FRAME).astype(np.float32).astype(ml_dtypes.bfloat16)


def chip_order():
    offsets = list(itertools.product(range(4), repeat=3))[1:]
    orbits, seen = [], set()
    for start in offsets:
        if start in seen:
            continue
        orbit, now = [], start
        for _ in range(3):
            for one in (now, tuple((4 - v) % 4 for v in now)):
                if one not in orbit:
                    orbit.append(one)
            now = (now[1], now[2], now[0])
        seen.update(orbit)
        orbits.append(orbit)
    mixed = np.random.RandomState(1).permutation(len(orbits))
    return [o for i in mixed for o in orbits[i]] + [(0, 0, 0)]


ORDER = chip_order()


def channelize(volt, window, table, out, raw, filtered, taps, whole, rows, spectra, sendbuf, raw_sem, row_sem, send_sem, recv_sem, own_sem):
    row, column = lax.axis_index("inp"), lax.axis_index("tm")
    x, y, z, core = column // 4, row // 2, (row % 2) * 2 + (column // 2) % 2, column % 2
    me = row * 16 + column

    cuts = [(0, HALF + TAPS - 1), (HALF + TAPS - 1, FRAMES + TAPS - 1)]
    loads = []
    for h, (lo, hi) in enumerate(cuts):
        for i in range(INPUTS // 16):
            at = (pl.ds(16 * i, 16), pl.ds(lo * FRAME, (hi - lo) * FRAME))
            loads.append(pltpu.make_async_copy(volt.at[at], raw.at[at], raw_sem.at[h, i]))
    small = [
        pltpu.make_async_copy(window, taps, row_sem.at[0]),
        pltpu.make_async_copy(table, whole, row_sem.at[1]),
    ]
    for load in small[:1] + loads[:4] + small[1:] + loads[4:]:
        load.start()

    barrier = pltpu.get_barrier_semaphore()

    def greet(step, carry):
        other = lax.rem(me + step, 128)
        pl.semaphore_signal(barrier, inc=1, device_id=(other // 16, other % 16), device_id_type=MESH)
        return carry

    lax.fori_loop(1, 128, greet, 0)
    small[0].wait()

    copies = []
    for h in range(2):
        for i in range(INPUTS // 16):
            loads[4 * h + i].wait()

            def filter_tile(j, carry, i=i, h=h):
                at = pl.multiple_of(j * 128, 128)
                weight = [taps[pl.ds(k, 1), pl.ds(at, 128)] for k in range(TAPS)]
                held = []
                for f in range(HALF * h, HALF * h + HALF + TAPS - 1):
                    held.append(raw[pl.ds(16 * i, 16), pl.ds(f * FRAME + at, 128)].astype(jnp.float32))
                    if len(held) == TAPS:
                        total = weight[0] * held[0]
                        for k in range(1, TAPS):
                            total = total + weight[k] * held[k]
                        held.pop(0)
                        g = f - TAPS + 1
                        filtered[pl.ds(g * INPUTS + 16 * i, 16), pl.ds(at, 128)] = total.astype(jnp.bfloat16)
                return carry

            lax.fori_loop(0, FRAME // 128, filter_tile, 0)
        if h == 0:
            small[1].wait()

        for chunk in range(CHIPS // CHUNK):
            units = range(chunk * CHUNK, (chunk + 1) * CHUNK)
            places = []
            for k in units:
                dx, dy, dz = ORDER[k]
                px, py, pz = lax.rem(x + dx, 4), lax.rem(y + dy, 4), lax.rem(z + dz, 4)
                inp, tm = py * 2 + pz // 2, px * 4 + lax.rem(pz, 2) * 2
                places.append((inp, tm))
                if h == 0:
                    chip = inp * 8 + tm // 2
                    rows[k * UNIT : (k + 1) * UNIT, :] = whole[pl.ds(pl.multiple_of(chip * UNIT, UNIT), UNIT), :]
            product = lax.dot_general(
                rows[chunk * ROWS : (chunk + 1) * ROWS, :],
                filtered[h * HALF * INPUTS : (h + 1) * HALF * INPUTS, :],
                (((1,), (1,)), ((), ())),
                preferred_element_type=jnp.float32,
            )
            for n in range(PAIRS):
                spectra[n * PITCH : n * PITCH + ROWS, :] = product[:, n * 128 : (n + 1) * 128]

            def gather(u, carry, chunk=chunk, h=h):
                for r in range(UNIT // 2):
                    pair = [spectra[pl.ds(u * UNIT + 2 * r + p, PAIRS, stride=PITCH), :] for p in range(2)]
                    sendbuf[h, chunk * CHUNK + u, r] = jnp.concatenate(pair, axis=0).astype(jnp.bfloat16)
                return carry

            lax.fori_loop(0, CHUNK, gather, 0)

            if h == 0 and chunk == 0:
                pl.semaphore_wait(barrier, 127)
            for k in units:
                inp, tm = places[k - units.start]
                for turn in range(2):
                    to = lax.rem(core + turn, 2)
                    part = sendbuf.at[h, k, pl.ds(to * 4, 4)]
                    if ORDER[k] == (0, 0, 0) and turn == 0:
                        copy = pltpu.make_async_copy(part, out.at[h, me], own_sem.at[h])
                    else:
                        copy = pltpu.make_async_remote_copy(
                            src_ref=part,
                            dst_ref=out.at[h, me],
                            send_sem=send_sem.at[h, k, turn],
                            recv_sem=recv_sem.at[h, k, turn],
                            device_id=(inp, tm + to),
                            device_id_type=MESH,
                        )
                    copy.start()
                    copies.append(copy)
    for copy in copies:
        copy.wait()


def correlate(block, out, held, turned, made, in_sem, out_sem):
    loads = [pltpu.make_async_copy(block.at[:, :, c], held.at[c], in_sem.at[c]) for c in range(4)]
    for load in loads:
        load.start()
    nt = (((1,), (1,)), ((), ()))
    same = lax.broadcasted_iota(jnp.int32, (128, 128), 0) == lax.broadcasted_iota(jnp.int32, (128, 128), 1)

    def scale(power):
        return lax.rsqrt(power * (LIFT**-2 / TOTAL) + 1e-06) * (1.0 / LIFT)

    stores = []
    for c in range(4):
        s = c % 2
        loads[c].wait()
        for p in range(2):
            for h in range(2):
                for k in range(4):
                    even = held[c, h, 32 * k : 32 * k + 16, 8 * p : 8 * p + 8, :].reshape(128, 128)
                    odd = held[c, h, 32 * k + 16 : 32 * k + 32, 8 * p : 8 * p + 8, :].reshape(128, 128)
                    for f in range(2):
                        cut = slice(64 * f, 64 * f + 64)
                        tile = jnp.concatenate([even[:, cut], odd[:, cut]], axis=1)
                        at = 512 * p + 256 * h + 128 * f
                        turned[s, 128 * k : 128 * k + 128, at : at + 128] = tile.T

        def dot(a, b, s=s):
            left, right = [
                turned[s, 256 * i : 256 * i + 256, :]
                if p is None
                else turned[s, 256 * i : 256 * i + 256, 512 * p : 512 * p + 512]
                for i, p in (a, b)
            ]
            return lax.dot_general(left, right, nt, preferred_element_type=jnp.float32)

        if c >= 2:
            for store in stores[2 * c - 4 : 2 * c - 2]:
                store.wait()
        own = [dot((i, None), (i, None)) for i in range(2)]
        along, down = [], []
        for block_sum in own:
            tiles = [
                jnp.where(same, block_sum[128 * k : 128 * k + 128, 128 * k : 128 * k + 128], 0.0) for k in range(2)
            ]
            along.append(
                scale(jnp.concatenate([jnp.sum(t, axis=0, keepdims=True) for t in tiles], axis=1)) * (1.0 / TOTAL)
            )
            down.append(scale(jnp.concatenate([jnp.sum(t, axis=1, keepdims=True) for t in tiles], axis=0)))
        for i in range(2):
            cut = slice(256 * i, 256 * i + 256)
            made[s, 0, cut, cut] = own[i] * along[i] * down[i]
        mixed = dot((0, None), (1, None)) * along[1] * down[0]
        made[s, 0, 0:256, 256:512] = mixed
        made[s, 0, 256:512, 0:256] = mixed.T
        stores.append(pltpu.make_async_copy(made.at[s, 0], out.at[c, 0], out_sem.at[s, 0]))
        stores[-1].start()
        for i in range(2):
            cut = slice(256 * i, 256 * i + 256)
            cross = dot((i, 1), (i, 0))
            made[s, 1, cut, cut] = (cross - cross.T) * along[i] * down[i]
        mixed = (dot((0, 1), (1, 0)) - dot((0, 0), (1, 1))) * along[1] * down[0]
        made[s, 1, 0:256, 256:512] = mixed
        made[s, 1, 256:512, 0:256] = -mixed.T
        stores.append(pltpu.make_async_copy(made.at[s, 1], out.at[c, 1], out_sem.at[s, 1]))
        stores[-1].start()
    for store in stores[4:]:
        store.wait()


def on_device(volt):
    whole = pl.BlockSpec(memory_space=pl.ANY)
    block = pl.pallas_call(
        channelize,
        out_shape=jax.ShapeDtypeStruct((2, 128, 4, 16, 128), jnp.bfloat16),
        in_specs=[whole, whole, whole],
        out_specs=whole,
        scratch_shapes=[
            pltpu.VMEM((INPUTS, (FRAMES + TAPS - 1) * FRAME), jnp.bfloat16),
            pltpu.VMEM((FRAMES * INPUTS, FRAME), jnp.bfloat16),
            pltpu.VMEM((TAPS, FRAME), jnp.float32),
            pltpu.VMEM((CHIPS * UNIT, FRAME), jnp.bfloat16),
            pltpu.VMEM((CHIPS * UNIT, FRAME), jnp.bfloat16),
            pltpu.VMEM((PAIRS * PITCH, 128), jnp.float32),
            pltpu.VMEM((2, CHIPS, 8, 16, 128), jnp.bfloat16),
            pltpu.SemaphoreType.DMA((2, INPUTS // 16)),
            pltpu.SemaphoreType.DMA((2,)),
            pltpu.SemaphoreType.DMA((2, CHIPS, 2)),
            pltpu.SemaphoreType.DMA((2, CHIPS, 2)),
            pltpu.SemaphoreType.DMA((2,)),
        ],
        compiler_params=pltpu.CompilerParams(
            collective_id=0, has_side_effects=True, vmem_limit_bytes=60 << 20
        ),
        name="channelize",
    )(volt, jnp.asarray(window_table()), jnp.asarray(twiddle_table()))
    return pl.pallas_call(
        correlate,
        out_shape=jax.ShapeDtypeStruct((4, 2, 512, 512), jnp.float32),
        in_specs=[whole],
        out_specs=whole,
        scratch_shapes=[
            pltpu.VMEM((4, 2, 128, 16, 128), jnp.bfloat16),
            pltpu.VMEM((2, 512, 1024), jnp.bfloat16),
            pltpu.VMEM((2, 2, 512, 512), jnp.float32),
            pltpu.SemaphoreType.DMA((4,)),
            pltpu.SemaphoreType.DMA((2, 2)),
        ],
        compiler_params=pltpu.CompilerParams(vmem_limit_bytes=60 << 20),
        name="correlate",
    )(block)


def solution(mesh):
    return jax.shard_map(
        on_device,
        mesh=mesh,
        in_specs=(P("inp", "tm"),),
        out_specs=P(("inp", "tm"), None, None, None),
        check_vma=False,
    )
```

time: 83.1 us -> 76.6 us (0.922)
  local copies, waits for them, and re-layouts: 4.49 us -> 0 us
  Pallas kernels: 78.3 us -> 76.3 us
    unnamed x6 -> x0, local copies, waits for them, and re-layouts: 4.49 us -> none
    pallas_call x2, Pallas kernels: 78.3 us -> 76.3 us  [the longest x1 65.1 us: on_device(): pl.pallas_call(channelize, out_shape=jax.ShapeDtypeStruct((2, 128, 4, 16,...]
where the time goes in v1:
time: 76.6 us; the launch traced here: 76.5 us
  Pallas kernels  76.3 us (100%)
    pallas_call x1, Pallas kernels, on_device(): pl.pallas_call(channelize, out_shape=jax.ShapeDtypeStruct((2, 128, 4, 16,...  65.1 us
    pallas_call x1, Pallas kernels, on_device(): pl.pallas_call(correlate, out_shape=jax.ShapeDtypeStruct((4, 2, 512, 512)...  11.2 us

profile of v1, /device:TPU:1, one launch (start us, length us, event | category | flops | bytes accessed | tf_op | source)
XLA Modules:
  0.0 76.5 jit_solution(3008850734752584166)
XLA Ops:
  0.0 65.1 %channelize.1.block = bf16[2,128,4,16,128]{4,3,2,1,0:T(8,128)(2,1)} custom-call(bf16[64,35840]{1,0:T(8,128)(2,1)} %volt.1, f32[4,1024]{1,0:T(4,128)} %constant.4.clone.window, bf16[1024,1024]{1,0:T(8,128)(2,1)} %constant.5.clone.table), custom_call_target="tpu_custom_call" | custom-call | tf_op jit(solution)/shard_map/channelize/pallas_call | solution.py:240
  65.1 11.2 %correlate.1 = f32[4,2,512,512]{3,2,1,0:T(8,128)} custom-call(bf16[2,128,4,16,128]{4,3,2,1,0:T(8,128)(2,1)} %channelize.1.block), custom_call_target="tpu_custom_call" | custom-call | tf_op jit(solution)/shard_map/correlate/pallas_call | solution.py:264

commit v2 on v1

--- a/solution.py
+++ b/solution.py
@@ -81,17 +81,29 @@
     for load in small[:1] + loads[:4] + small[1:] + loads[4:]:
         load.start()
 
+    def onward(at, step):
+        there = at + step
+        return jnp.where(there >= 4, there - 4, there)
+
+    xs = [onward(x, d) * 4 for d in range(4)]
+    ys = [onward(y, d) * 2 for d in range(4)]
+    upper = [jnp.where(onward(z, d) >= 2, 1, 0) for d in range(4)]
+    lower = [(onward(z, d) - 2 * upper[d]) * 2 for d in range(4)]
+    cores = [core, 1 - core]
+
+    def chip_at(offset):
+        dx, dy, dz = offset
+        return ys[dy] + upper[dz], xs[dx] + lower[dz]
+
     barrier = pltpu.get_barrier_semaphore()
-
-    def greet(step, carry):
-        other = lax.rem(me + step, 128)
-        pl.semaphore_signal(barrier, inc=1, device_id=(other // 16, other % 16), device_id_type=MESH)
-        return carry
-
-    lax.fori_loop(1, 128, greet, 0)
+    for offset in ORDER:
+        inp, tm = chip_at(offset)
+        for turn in range(2):
+            if (offset, turn) != ((0, 0, 0), 0):
+                pl.semaphore_signal(barrier, inc=1, device_id=(inp, tm + cores[turn]), device_id_type=MESH)
     small[0].wait()
 
-    copies = []
+    own = []
     for h in range(2):
         for i in range(INPUTS // 16):
             loads[4 * h + i].wait()
@@ -117,15 +129,11 @@
 
         for chunk in range(CHIPS // CHUNK):
             units = range(chunk * CHUNK, (chunk + 1) * CHUNK)
-            places = []
-            for k in units:
-                dx, dy, dz = ORDER[k]
-                px, py, pz = lax.rem(x + dx, 4), lax.rem(y + dy, 4), lax.rem(z + dz, 4)
-                inp, tm = py * 2 + pz // 2, px * 4 + lax.rem(pz, 2) * 2
-                places.append((inp, tm))
-                if h == 0:
-                    chip = inp * 8 + tm // 2
-                    rows[k * UNIT : (k + 1) * UNIT, :] = whole[pl.ds(pl.multiple_of(chip * UNIT, UNIT), UNIT), :]
+            if h == 0:
+                for k in units:
+                    inp, tm = chip_at(ORDER[k])
+                    at = pl.multiple_of(inp * (8 * UNIT) + tm * (UNIT // 2), UNIT)
+                    rows[k * UNIT : (k + 1) * UNIT, :] = whole[pl.ds(at, UNIT), :]
             product = lax.dot_general(
                 rows[chunk * ROWS : (chunk + 1) * ROWS, :],
                 filtered[h * HALF * INPUTS : (h + 1) * HALF * INPUTS, :],
@@ -138,7 +146,7 @@
             def gather(u, carry, chunk=chunk, h=h):
                 for r in range(UNIT // 2):
                     pair = [spectra[pl.ds(u * UNIT + 2 * r + p, PAIRS, stride=PITCH), :] for p in range(2)]
-                    sendbuf[h, chunk * CHUNK + u, r] = jnp.concatenate(pair, axis=0).astype(jnp.bfloat16)
+                    sendbuf[h, 2 * (chunk * CHUNK + u) + r // 4, r % 4] = jnp.concatenate(pair, axis=0).astype(jnp.bfloat16)
                 return carry
 
             lax.fori_loop(0, CHUNK, gather, 0)
@@ -146,25 +154,34 @@
             if h == 0 and chunk == 0:
                 pl.semaphore_wait(barrier, 127)
             for k in units:
-                inp, tm = places[k - units.start]
+                inp, tm = chip_at(ORDER[k])
                 for turn in range(2):
-                    to = lax.rem(core + turn, 2)
-                    part = sendbuf.at[h, k, pl.ds(to * 4, 4)]
+                    to = cores[turn]
+                    part = sendbuf.at[h, 2 * k + to]
                     if ORDER[k] == (0, 0, 0) and turn == 0:
                         copy = pltpu.make_async_copy(part, out.at[h, me], own_sem.at[h])
+                        own.append(copy)
                     else:
                         copy = pltpu.make_async_remote_copy(
                             src_ref=part,
                             dst_ref=out.at[h, me],
-                            send_sem=send_sem.at[h, k, turn],
-                            recv_sem=recv_sem.at[h, k, turn],
+                            send_sem=send_sem.at[h],
+                            recv_sem=recv_sem.at[h],
                             device_id=(inp, tm + to),
                             device_id_type=MESH,
                         )
                     copy.start()
-                    copies.append(copy)
-    for copy in copies:
-        copy.wait()
+    for h in range(2):
+        own[h].wait()
+        every = pltpu.make_async_remote_copy(
+            src_ref=sendbuf.at[h, pl.ds(0, 127)],
+            dst_ref=out.at[h, pl.ds(0, 127)],
+            send_sem=send_sem.at[h],
+            recv_sem=recv_sem.at[h],
+            device_id=(row, column - core + cores[1]),
+            device_id_type=MESH,
+        )
+        every.wait()
 
 
 def correlate(block, out, held, turned, made, in_sem, out_sem):
@@ -183,14 +200,11 @@
         loads[c].wait()
         for p in range(2):
             for h in range(2):
-                for k in range(4):
-                    even = held[c, h, 32 * k : 32 * k + 16, 8 * p : 8 * p + 8, :].reshape(128, 128)
-                    odd = held[c, h, 32 * k + 16 : 32 * k + 32, 8 * p : 8 * p + 8, :].reshape(128, 128)
+                for i in range(8):
+                    tile = held[c, h, 16 * i : 16 * i + 16, 8 * p : 8 * p + 8, :].reshape(128, 128).T
                     for f in range(2):
-                        cut = slice(64 * f, 64 * f + 64)
-                        tile = jnp.concatenate([even[:, cut], odd[:, cut]], axis=1)
                         at = 512 * p + 256 * h + 128 * f
-                        turned[s, 128 * k : 128 * k + 128, at : at + 128] = tile.T
+                        turned[s, 64 * i : 64 * i + 64, at : at + 128] = tile[64 * f : 64 * f + 64, :]
 
         def dot(a, b, s=s):
             left, right = [
@@ -249,11 +263,11 @@
             pltpu.VMEM((CHIPS * UNIT, FRAME), jnp.bfloat16),
             pltpu.VMEM((CHIPS * UNIT, FRAME), jnp.bfloat16),
             pltpu.VMEM((PAIRS * PITCH, 128), jnp.float32),
-            pltpu.VMEM((2, CHIPS, 8, 16, 128), jnp.bfloat16),
+            pltpu.VMEM((2, 2 * CHIPS, 4, 16, 128), jnp.bfloat16),
             pltpu.SemaphoreType.DMA((2, INPUTS // 16)),
             pltpu.SemaphoreType.DMA((2,)),
-            pltpu.SemaphoreType.DMA((2, CHIPS, 2)),
-            pltpu.SemaphoreType.DMA((2, CHIPS, 2)),
+            pltpu.SemaphoreType.DMA((2,)),
+            pltpu.SemaphoreType.DMA((2,)),
             pltpu.SemaphoreType.DMA((2,)),
         ],
         compiler_params=pltpu.CompilerParams(

time: 76.6 us -> 67.4 us (0.88)
  Pallas kernels: 76.3 us -> 67.3 us
    pallas_call x1, Pallas kernels: 65.1 us -> 59.6 us  [on_device(): pl.pallas_call(channelize, out_shape=jax.ShapeDtypeStruct((2, 128, 4, 16,...]
    pallas_call x1, Pallas kernels: 11.2 us -> 7.71 us  [on_device(): pl.pallas_call(correlate, out_shape=jax.ShapeDtypeStruct((4, 2, 512, 512)...]
where the time goes in v2:
time: 67.4 us; the launch traced here: 67.3 us
  Pallas kernels  67.3 us (100%)
    pallas_call x1, Pallas kernels, on_device(): pl.pallas_call(channelize, out_shape=jax.ShapeDtypeStruct((2, 128, 4, 16,...  59.6 us
    pallas_call x1, Pallas kernels, on_device(): pl.pallas_call(correlate, out_shape=jax.ShapeDtypeStruct((4, 2, 512, 512)...  7.71 us

profile of v2, /device:TPU:1, one launch (start us, length us, event | category | flops | bytes accessed | tf_op | source)
XLA Modules:
  0.0 67.3 jit_solution(17985023234386475345)
XLA Ops:
  0.0 59.6 %channelize.1.block = bf16[2,128,4,16,128]{4,3,2,1,0:T(8,128)(2,1)} custom-call(bf16[64,35840]{1,0:T(8,128)(2,1)} %volt.1, f32[4,1024]{1,0:T(4,128)} %constant.4.clone.window, bf16[1024,1024]{1,0:T(8,128)(2,1)} %constant.5.clone.table), custom_call_target="tpu_custom_call" | custom-call | tf_op jit(solution)/shard_map/channelize/pallas_call | solution.py:254
  59.6 7.7 %correlate.1 = f32[4,2,512,512]{3,2,1,0:T(8,128)} custom-call(bf16[2,128,4,16,128]{4,3,2,1,0:T(8,128)(2,1)} %channelize.1.block), custom_call_target="tpu_custom_call" | custom-call | tf_op jit(solution)/shard_map/correlate/pallas_call | solution.py:278

commit v3 on v2

--- a/solution.py
+++ b/solution.py
@@ -42,7 +42,7 @@
     return pair.reshape(2 * chans, FRAME).astype(np.float32).astype(ml_dtypes.bfloat16)
 
 
-def chip_order():
+def chip_orders():
     offsets = list(itertools.product(range(4), repeat=3))[1:]
     orbits, seen = [], set()
     for start in offsets:
@@ -56,11 +56,12 @@
             now = (now[1], now[2], now[0])
         seen.update(orbit)
         orbits.append(orbit)
-    mixed = np.random.RandomState(1).permutation(len(orbits))
-    return [o for i in mixed for o in orbits[i]] + [(0, 0, 0)]
-
-
-ORDER = chip_order()
+    mixed = [orbits[i] for i in np.random.RandomState(1).permutation(len(orbits))]
+    falling = sorted(orbits, key=lambda orbit: -sum(min(v, 4 - v) for v in orbit[0]))
+    return [[o for orbit in order for o in orbit] + [(0, 0, 0)] for order in (mixed, falling)]
+
+
+ORDERS = chip_orders()
 
 
 def channelize(volt, window, table, out, raw, filtered, taps, whole, rows, spectra, sendbuf, raw_sem, row_sem, send_sem, recv_sem, own_sem):
@@ -96,7 +97,7 @@
         return ys[dy] + upper[dz], xs[dx] + lower[dz]
 
     barrier = pltpu.get_barrier_semaphore()
-    for offset in ORDER:
+    for offset in ORDERS[0]:
         inp, tm = chip_at(offset)
         for turn in range(2):
             if (offset, turn) != ((0, 0, 0), 0):
@@ -129,11 +130,10 @@
 
         for chunk in range(CHIPS // CHUNK):
             units = range(chunk * CHUNK, (chunk + 1) * CHUNK)
-            if h == 0:
-                for k in units:
-                    inp, tm = chip_at(ORDER[k])
-                    at = pl.multiple_of(inp * (8 * UNIT) + tm * (UNIT // 2), UNIT)
-                    rows[k * UNIT : (k + 1) * UNIT, :] = whole[pl.ds(at, UNIT), :]
+            for k in units:
+                inp, tm = chip_at(ORDERS[h][k])
+                at = pl.multiple_of(inp * (8 * UNIT) + tm * (UNIT // 2), UNIT)
+                rows[k * UNIT : (k + 1) * UNIT, :] = whole[pl.ds(at, UNIT), :]
             product = lax.dot_general(
                 rows[chunk * ROWS : (chunk + 1) * ROWS, :],
                 filtered[h * HALF * INPUTS : (h + 1) * HALF * INPUTS, :],
@@ -154,11 +154,11 @@
             if h == 0 and chunk == 0:
                 pl.semaphore_wait(barrier, 127)
             for k in units:
-                inp, tm = chip_at(ORDER[k])
+                inp, tm = chip_at(ORDERS[h][k])
                 for turn in range(2):
                     to = cores[turn]
                     part = sendbuf.at[h, 2 * k + to]
-                    if ORDER[k] == (0, 0, 0) and turn == 0:
+                    if ORDERS[h][k] == (0, 0, 0) and turn == 0:
                         copy = pltpu.make_async_copy(part, out.at[h, me], own_sem.at[h])
                         own.append(copy)
                     else:
@@ -185,26 +185,40 @@
 
 
 def correlate(block, out, held, turned, made, in_sem, out_sem):
-    loads = [pltpu.make_async_copy(block.at[:, :, c], held.at[c], in_sem.at[c]) for c in range(4)]
-    for load in loads:
-        load.start()
+    loads = [
+        [pltpu.make_async_copy(block.at[h, :, c], held.at[c, h], in_sem.at[c, h]) for h in range(2)] for c in range(4)
+    ]
     nt = (((1,), (1,)), ((), ()))
     same = lax.broadcasted_iota(jnp.int32, (128, 128), 0) == lax.broadcasted_iota(jnp.int32, (128, 128), 1)
 
     def scale(power):
         return lax.rsqrt(power * (LIFT**-2 / TOTAL) + 1e-06) * (1.0 / LIFT)
 
+    def turn(c, h):
+        for p in range(2):
+            for i in range(8):
+                tile = held[c, h, 16 * i : 16 * i + 16, 8 * p : 8 * p + 8, :].reshape(128, 128).T
+                for f in range(2):
+                    at = 512 * p + 256 * h + 128 * f
+                    turned[c % 2, 64 * i : 64 * i + 64, at : at + 128] = tile[64 * f : 64 * f + 64, :]
+
+    def store(c, p, rows, first):
+        stores.append(
+            pltpu.make_async_copy(
+                made.at[c, p, pl.ds(first, rows)], out.at[c, p, pl.ds(first, rows)], out_sem.at[c, p, first // 256]
+            )
+        )
+        stores[-1].start()
+
     stores = []
     for c in range(4):
+        for h in range(2):
+            loads[c][h].start()
+    for h in range(2):
+        loads[0][h].wait()
+        turn(0, h)
+    for c in range(4):
         s = c % 2
-        loads[c].wait()
-        for p in range(2):
-            for h in range(2):
-                for i in range(8):
-                    tile = held[c, h, 16 * i : 16 * i + 16, 8 * p : 8 * p + 8, :].reshape(128, 128).T
-                    for f in range(2):
-                        at = 512 * p + 256 * h + 128 * f
-                        turned[s, 64 * i : 64 * i + 64, at : at + 128] = tile[64 * f : 64 * f + 64, :]
 
         def dot(a, b, s=s):
             left, right = [
@@ -215,38 +229,35 @@
             ]
             return lax.dot_general(left, right, nt, preferred_element_type=jnp.float32)
 
-        if c >= 2:
-            for store in stores[2 * c - 4 : 2 * c - 2]:
-                store.wait()
-        own = [dot((i, None), (i, None)) for i in range(2)]
+        if c + 1 < 4:
+            for h in range(2):
+                loads[c + 1][h].wait()
+            for h in range(2):
+                turn(c + 1, h)
         along, down = [], []
-        for block_sum in own:
-            tiles = [
-                jnp.where(same, block_sum[128 * k : 128 * k + 128, 128 * k : 128 * k + 128], 0.0) for k in range(2)
-            ]
+        for i in range(2):
+            cut = slice(256 * i, 256 * i + 256)
+            total = dot((i, None), (i, None))
+            tiles = [jnp.where(same, total[128 * k : 128 * k + 128, 128 * k : 128 * k + 128], 0.0) for k in range(2)]
             along.append(
                 scale(jnp.concatenate([jnp.sum(t, axis=0, keepdims=True) for t in tiles], axis=1)) * (1.0 / TOTAL)
             )
             down.append(scale(jnp.concatenate([jnp.sum(t, axis=1, keepdims=True) for t in tiles], axis=0)))
-        for i in range(2):
-            cut = slice(256 * i, 256 * i + 256)
-            made[s, 0, cut, cut] = own[i] * along[i] * down[i]
+            made[c, 0, cut, cut] = total * along[i] * down[i]
         mixed = dot((0, None), (1, None)) * along[1] * down[0]
-        made[s, 0, 0:256, 256:512] = mixed
-        made[s, 0, 256:512, 0:256] = mixed.T
-        stores.append(pltpu.make_async_copy(made.at[s, 0], out.at[c, 0], out_sem.at[s, 0]))
-        stores[-1].start()
+        made[c, 0, 0:256, 256:512] = mixed
+        made[c, 0, 256:512, 0:256] = mixed.T
+        store(c, 0, 512, 0)
+        mixed = (dot((0, 1), (1, 0)) - dot((0, 0), (1, 1))) * along[1] * down[0]
+        made[c, 1, 0:256, 256:512] = mixed
+        made[c, 1, 256:512, 0:256] = -mixed.T
         for i in range(2):
             cut = slice(256 * i, 256 * i + 256)
             cross = dot((i, 1), (i, 0))
-            made[s, 1, cut, cut] = (cross - cross.T) * along[i] * down[i]
-        mixed = (dot((0, 1), (1, 0)) - dot((0, 0), (1, 1))) * along[1] * down[0]
-        made[s, 1, 0:256, 256:512] = mixed
-        made[s, 1, 256:512, 0:256] = -mixed.T
-        stores.append(pltpu.make_async_copy(made.at[s, 1], out.at[c, 1], out_sem.at[s, 1]))
-        stores[-1].start()
-    for store in stores[4:]:
-        store.wait()
+            made[c, 1, cut, cut] = (cross - cross.T) * along[i] * down[i]
+            store(c, 1, 256, 256 * i)
+    for one in stores:
+        one.wait()
 
 
 def on_device(volt):
@@ -283,9 +294,9 @@
         scratch_shapes=[
             pltpu.VMEM((4, 2, 128, 16, 128), jnp.bfloat16),
             pltpu.VMEM((2, 512, 1024), jnp.bfloat16),
-            pltpu.VMEM((2, 2, 512, 512), jnp.float32),
-            pltpu.SemaphoreType.DMA((4,)),
-            pltpu.SemaphoreType.DMA((2, 2)),
+            pltpu.VMEM((4, 2, 512, 512), jnp.float32),
+            pltpu.SemaphoreType.DMA((4, 2)),
+            pltpu.SemaphoreType.DMA((4, 2, 2)),
         ],
         compiler_params=pltpu.CompilerParams(vmem_limit_bytes=60 << 20),
         name="correlate",

time: 67.4 us -> 65.8 us (0.976)
  Pallas kernels: 67.3 us -> 65.7 us
    pallas_call x1, Pallas kernels: 59.6 us -> 58.7 us  [on_device(): pl.pallas_call(channelize, out_shape=jax.ShapeDtypeStruct((2, 128, 4, 16,...]
    pallas_call x1, Pallas kernels: 7.71 us -> 7 us  [on_device(): pl.pallas_call(correlate, out_shape=jax.ShapeDtypeStruct((4, 2, 512, 512)...]
where the time goes in v3:
time: 65.8 us; the launch traced here: 65.7 us
  Pallas kernels  65.7 us (100%)
    pallas_call x1, Pallas kernels, on_device(): pl.pallas_call(channelize, out_shape=jax.ShapeDtypeStruct((2, 128, 4, 16,...  58.7 us
    pallas_call x1, Pallas kernels, on_device(): pl.pallas_call(correlate, out_shape=jax.ShapeDtypeStruct((4, 2, 512, 512)...  7 us

profile of v3, /device:TPU:1, one launch (start us, length us, event | category | flops | bytes accessed | tf_op | source)
XLA Modules:
  0.0 65.7 jit_solution(3334212984617324491)
XLA Ops:
  0.0 58.7 %channelize.1.block = bf16[2,128,4,16,128]{4,3,2,1,0:T(8,128)(2,1)} custom-call(bf16[64,35840]{1,0:T(8,128)(2,1)} %volt.1, f32[4,1024]{1,0:T(4,128)} %constant.4.clone.window, bf16[1024,1024]{1,0:T(8,128)(2,1)} %constant.5.clone.table), custom_call_target="tpu_custom_call" | custom-call | tf_op jit(solution)/shard_map/channelize/pallas_call | solution.py:265
  58.7 7.0 %correlate.1 = f32[4,2,512,512]{3,2,1,0:T(8,128)} custom-call(bf16[2,128,4,16,128]{4,3,2,1,0:T(8,128)(2,1)} %channelize.1.block), custom_call_target="tpu_custom_call" | custom-call | tf_op jit(solution)/shard_map/correlate/pallas_call | solution.py:289

commit v4 on v2

v4 whole, which is shorter than its diff:
```python
import functools
import itertools

import jax
import jax.numpy as jnp
import ml_dtypes
import numpy as np
from jax import lax
from jax.experimental import pallas as pl
from jax.experimental.pallas import tpu as pltpu
from jax.sharding import PartitionSpec as P

MESH = pl.DeviceIdType.MESH
FRAME = 1024
TAPS = 4
INPUTS = 64
FRAMES = 32
HALF = 16
PAIRS = 8
CHIPS = 64
UNIT = 16
CHUNK = 16
ROWS = CHUNK * UNIT
PITCH = ROWS + 8
TOTAL = 512
LIFT = 2.0**32


def window_table():
    index = np.arange(TAPS * FRAME, dtype=np.float64)
    shifted = (index - TAPS * FRAME / 2 + 0.5) / FRAME
    shaped = np.sinc(shifted) * (0.54 - 0.46 * np.cos(2.0 * np.pi * index / (TAPS * FRAME - 1)))
    return (shaped.reshape(TAPS, FRAME) * LIFT).astype(np.float32)


def twiddle_table():
    chans = FRAME // 2
    turn = np.arange(chans)[:, None] * np.arange(FRAME)[None, :] % FRAME
    phase = turn.astype(np.float32) * np.float32(2.0 * np.pi / FRAME)
    phase = phase.astype(np.float64)
    pair = np.stack([np.cos(phase), -np.sin(phase)], axis=1)
    return pair.reshape(2 * chans, FRAME).astype(np.float32).astype(ml_dtypes.bfloat16)


def chip_orders():
    offsets = list(itertools.product(range(4), repeat=3))[1:]
    orbits, seen = [], set()
    for start in offsets:
        if start in seen:
            continue
        orbit, now = [], start
        for _ in range(3):
            for one in (now, tuple((4 - v) % 4 for v in now)):
                if one not in orbit:
                    orbit.append(one)
            now = (now[1], now[2], now[0])
        seen.update(orbit)
        orbits.append(orbit)
    mixed = [orbits[i] for i in np.random.RandomState(1).permutation(len(orbits))]
    falling = sorted(orbits, key=lambda orbit: -sum(min(v, 4 - v) for v in orbit[0]))
    return [[o for orbit in order for o in orbit] + [(0, 0, 0)] for order in (mixed, falling)]


ORDERS = chip_orders()


ROUNDS = [(0, 1, 0, 2), (1, 1, 0, 2), (0, 2, 2, 2)]


def turn(held, turned, h):
    for p in range(2):
        for i in range(8):
            tile = held[16 * i : 16 * i + 16, 8 * p : 8 * p + 8, :].reshape(128, 128).T
            for f in range(2):
                at = 512 * p + 256 * h + 128 * f
                turned[64 * i : 64 * i + 64, at : at + 128] = tile[64 * f : 64 * f + 64, :]


def products(turned, made, out, sem, stores):
    same = lax.broadcasted_iota(jnp.int32, (128, 128), 0) == lax.broadcasted_iota(jnp.int32, (128, 128), 1)

    def scale(power):
        return lax.rsqrt(power * (LIFT**-2 / TOTAL) + 1e-06) * (1.0 / LIFT)

    def dot(a, b):
        left, right = [
            turned[256 * i : 256 * i + 256, :]
            if p is None
            else turned[256 * i : 256 * i + 256, 512 * p : 512 * p + 512]
            for i, p in (a, b)
        ]
        return lax.dot_general(left, right, (((1,), (1,)), ((), ())), preferred_element_type=jnp.float32)

    def store(p, first, count):
        at = (p, pl.ds(first, count))
        stores.append(pltpu.make_async_copy(made.at[at], out.at[at], sem.at[p, first // 256]))
        stores[-1].start()

    along, down = [], []
    for i in range(2):
        cut = slice(256 * i, 256 * i + 256)
        total = dot((i, None), (i, None))
        tiles = [jnp.where(same, total[128 * k : 128 * k + 128, 128 * k : 128 * k + 128], 0.0) for k in range(2)]
        along.append(
            scale(jnp.concatenate([jnp.sum(t, axis=0, keepdims=True) for t in tiles], axis=1)) * (1.0 / TOTAL)
        )
        down.append(scale(jnp.concatenate([jnp.sum(t, axis=1, keepdims=True) for t in tiles], axis=0)))
        made[0, cut, cut] = total * along[i] * down[i]
    mixed = dot((0, None), (1, None)) * along[1] * down[0]
    made[0, 0:256, 256:512] = mixed
    made[0, 256:512, 0:256] = mixed.T
    store(0, 0, 512)
    mixed = (dot((0, 1), (1, 0)) - dot((0, 0), (1, 1))) * along[1] * down[0]
    made[1, 0:256, 256:512] = mixed
    made[1, 256:512, 0:256] = -mixed.T
    for i in range(2):
        cut = slice(256 * i, 256 * i + 256)
        cross = dot((i, 1), (i, 0))
        made[1, cut, cut] = (cross - cross.T) * along[i] * down[i]
        store(1, 256 * i, 256)


def channelize(
    volt, window, table, out, early,
    raw, filtered, taps, whole, rows, spectra, sendbuf, held, turned, made,
    raw_sem, row_sem, send_sem, recv_sem, own_sem, in_sem, out_sem,
):
    row, column = lax.axis_index("inp"), lax.axis_index("tm")
    x, y, z, core = column // 4, row // 2, (row % 2) * 2 + (column // 2) % 2, column % 2
    me = row * 16 + column

    cuts = [(0, HALF + TAPS - 1), (HALF + TAPS - 1, FRAMES + TAPS - 1)]
    loads = []
    for h, (lo, hi) in enumerate(cuts):
        for i in range(INPUTS // 16):
            at = (pl.ds(16 * i, 16), pl.ds(lo * FRAME, (hi - lo) * FRAME))
            loads.append(pltpu.make_async_copy(volt.at[at], raw.at[at], raw_sem.at[h, i]))
    small = [
        pltpu.make_async_copy(window, taps, row_sem.at[0]),
        pltpu.make_async_copy(table, whole, row_sem.at[1]),
    ]
    for load in small[:1] + loads[:4] + small[1:] + loads[4:]:
        load.start()

    def onward(at, step):
        there = at + step
        return jnp.where(there >= 4, there - 4, there)

    xs = [onward(x, d) * 4 for d in range(4)]
    ys = [onward(y, d) * 2 for d in range(4)]
    upper = [jnp.where(onward(z, d) >= 2, 1, 0) for d in range(4)]
    lower = [(onward(z, d) - 2 * upper[d]) * 2 for d in range(4)]
    cores = [core, 1 - core]

    def chip_at(offset):
        dx, dy, dz = offset
        return ys[dy] + upper[dz], xs[dx] + lower[dz]

    barrier = pltpu.get_barrier_semaphore()
    for offset in ORDERS[0]:
        inp, tm = chip_at(offset)
        for side in range(2):
            if (offset, side) != ((0, 0, 0), 0):
                pl.semaphore_signal(barrier, inc=1, device_id=(inp, tm + cores[side]), device_id_type=MESH)
    small[0].wait()

    def exchange(j):
        h, halves, lo, count = ROUNDS[j]
        at = (pl.ds(h, halves), pl.ds(0, 127), pl.ds(lo, count))
        return pltpu.make_async_remote_copy(
            src_ref=sendbuf.at[at],
            dst_ref=out.at[at],
            send_sem=send_sem.at[j],
            recv_sem=recv_sem.at[j],
            device_id=(row, column - core + cores[1]),
            device_id_type=MESH,
        )

    def arrive(j):
        own[j].wait()
        exchange(j).wait_recv()

    own = []

    def send(j, offsets):
        h, halves, lo, count = ROUNDS[j]
        for offset in offsets:
            inp, tm = chip_at(offset)
            k = ORDERS[0].index(offset)
            for side in range(2):
                to = cores[side]
                part = sendbuf.at[pl.ds(h, halves), 2 * k + to, pl.ds(lo, count)]
                there = out.at[pl.ds(h, halves), me, pl.ds(lo, count)]
                if offset == (0, 0, 0) and side == 0:
                    copy = pltpu.make_async_copy(part, there, own_sem.at[j])
                    own.append(copy)
                else:
                    copy = pltpu.make_async_remote_copy(
                        src_ref=part,
                        dst_ref=there,
                        send_sem=send_sem.at[j],
                        recv_sem=recv_sem.at[j],
                        device_id=(inp, tm + to),
                        device_id_type=MESH,
                    )
                copy.start()

    for h in range(2):
        for i in range(INPUTS // 16):
            loads[4 * h + i].wait()

            def filter_tile(j, carry, i=i, h=h):
                at = pl.multiple_of(j * 128, 128)
                weight = [taps[pl.ds(k, 1), pl.ds(at, 128)] for k in range(TAPS)]
                held = []
                for f in range(HALF * h, HALF * h + HALF + TAPS - 1):
                    held.append(raw[pl.ds(16 * i, 16), pl.ds(f * FRAME + at, 128)].astype(jnp.float32))
                    if len(held) == TAPS:
                        total = weight[0] * held[0]
                        for k in range(1, TAPS):
                            total = total + weight[k] * held[k]
                        held.pop(0)
                        g = f - TAPS + 1
                        filtered[pl.ds(g * INPUTS + 16 * i, 16), pl.ds(at, 128)] = total.astype(jnp.bfloat16)
                return carry

            lax.fori_loop(0, FRAME // 128, filter_tile, 0)
        if h == 0:
            small[1].wait()

        for chunk in range(CHIPS // CHUNK):
            units = range(chunk * CHUNK, (chunk + 1) * CHUNK)
            if h == 0:
                for k in units:
                    inp, tm = chip_at(ORDERS[0][k])
                    at = pl.multiple_of(inp * (8 * UNIT) + tm * (UNIT // 2), UNIT)
                    rows[k * UNIT : (k + 1) * UNIT, :] = whole[pl.ds(at, UNIT), :]
            product = lax.dot_general(
                rows[chunk * ROWS : (chunk + 1) * ROWS, :],
                filtered[h * HALF * INPUTS : (h + 1) * HALF * INPUTS, :],
                (((1,), (1,)), ((), ())),
                preferred_element_type=jnp.float32,
            )
            for n in range(PAIRS):
                spectra[n * PITCH : n * PITCH + ROWS, :] = product[:, n * 128 : (n + 1) * 128]

            def gather(u, carry, chunk=chunk, h=h):
                for r in range(UNIT // 2):
                    pair = [spectra[pl.ds(u * UNIT + 2 * r + p, PAIRS, stride=PITCH), :] for p in range(2)]
                    sendbuf[h, 2 * (chunk * CHUNK + u) + r // 4, r % 4] = jnp.concatenate(pair, axis=0).astype(jnp.bfloat16)
                return carry

            lax.fori_loop(0, CHUNK, gather, 0)

            if h == 0 and chunk == 0:
                pl.semaphore_wait(barrier, 127)
            send(h, ORDERS[0][units.start : units.stop])
    send(2, ORDERS[1])

    loads = [[pltpu.make_async_copy(out.at[h, :, c], held.at[c, h], in_sem.at[c, h]) for c in range(2)] for h in range(2)]
    for h in range(2):
        arrive(h)
        for load in loads[h]:
            load.start()
        for c in range(2):
            loads[h][c].wait()
            turn(held.at[c, h], turned.at[c], h)
    stores = []
    for c in range(2):
        products(turned.at[c], made.at[c], early.at[c], out_sem.at[c], stores)
    for store in stores:
        store.wait()
    arrive(2)
    for j in range(3):
        exchange(j).wait_send()


def correlate(block, early, out, held, turned, made, passed, in_sem, out_sem, early_sem):
    loads = [
        [pltpu.make_async_copy(block.at[h, :, c + 2], held.at[c, h], in_sem.at[c, h]) for h in range(2)]
        for c in range(2)
    ]
    moves = [pltpu.make_async_copy(early.at[c], passed.at[c], early_sem.at[c]) for c in range(2)]
    for load in loads[0] + moves + loads[1]:
        load.start()
    stores = []
    for h in range(2):
        loads[0][h].wait()
        turn(held.at[0, h], turned.at[0], h)
    for c in range(2):
        moves[c].wait()
        stores.append(pltpu.make_async_copy(passed.at[c], out.at[c], early_sem.at[c]))
        stores[-1].start()
    for h in range(2):
        loads[1][h].wait()
    for h in range(2):
        turn(held.at[1, h], turned.at[1], h)
    for c in range(2):
        products(turned.at[c], made.at[c], out.at[c + 2], out_sem.at[c], stores)
    for one in stores:
        one.wait()


def on_device(volt):
    whole = pl.BlockSpec(memory_space=pl.ANY)
    work = [
        pltpu.VMEM((2, 2, 128, 16, 128), jnp.bfloat16),
        pltpu.VMEM((2, 512, 1024), jnp.bfloat16),
        pltpu.VMEM((2, 2, 512, 512), jnp.float32),
    ]
    block, early = pl.pallas_call(
        channelize,
        out_shape=[
            jax.ShapeDtypeStruct((2, 128, 4, 16, 128), jnp.bfloat16),
            jax.ShapeDtypeStruct((2, 2, 512, 512), jnp.float32),
        ],
        in_specs=[whole] * 3,
        out_specs=[whole] * 2,
        scratch_shapes=[
            pltpu.VMEM((INPUTS, (FRAMES + TAPS - 1) * FRAME), jnp.bfloat16),
            pltpu.VMEM((FRAMES * INPUTS, FRAME), jnp.bfloat16),
            pltpu.VMEM((TAPS, FRAME), jnp.float32),
            pltpu.VMEM((CHIPS * UNIT, FRAME), jnp.bfloat16),
            pltpu.VMEM((CHIPS * UNIT, FRAME), jnp.bfloat16),
            pltpu.VMEM((PAIRS * PITCH, 128), jnp.float32),
            pltpu.VMEM((2, 2 * CHIPS, 4, 16, 128), jnp.bfloat16),
            *work,
            pltpu.SemaphoreType.DMA((2, INPUTS // 16)),
            pltpu.SemaphoreType.DMA((2,)),
            pltpu.SemaphoreType.DMA((3,)),
            pltpu.SemaphoreType.DMA((3,)),
            pltpu.SemaphoreType.DMA((3,)),
            pltpu.SemaphoreType.DMA((2, 2)),
            pltpu.SemaphoreType.DMA((2, 2, 2)),
        ],
        compiler_params=pltpu.CompilerParams(
            collective_id=0, has_side_effects=True, vmem_limit_bytes=60 << 20
        ),
        name="channelize",
    )(volt, jnp.asarray(window_table()), jnp.asarray(twiddle_table()))
    return pl.pallas_call(
        correlate,
        out_shape=jax.ShapeDtypeStruct((4, 2, 512, 512), jnp.float32),
        in_specs=[whole] * 2,
        out_specs=whole,
        scratch_shapes=[
            *work,
            pltpu.VMEM((2, 2, 512, 512), jnp.float32),
            pltpu.SemaphoreType.DMA((2, 2)),
            pltpu.SemaphoreType.DMA((2, 2, 2)),
            pltpu.SemaphoreType.DMA((2,)),
        ],
        compiler_params=pltpu.CompilerParams(vmem_limit_bytes=60 << 20),
        name="correlate",
    )(block, early)


def solution(mesh):
    return jax.shard_map(
        on_device,
        mesh=mesh,
        in_specs=(P("inp", "tm"),),
        out_specs=P(("inp", "tm"), None, None, None),
        check_vma=False,
    )
```

time: 67.4 us -> 65.4 us (0.970)
  Pallas kernels: 67.3 us -> 65.1 us
    pallas_call x1, Pallas kernels: 7.71 us -> 5.88 us  [on_device(): pl.pallas_call(correlate, out_shape=jax.ShapeDtypeStruct((4, 2, 512, 512)...]
where the time goes in v4:
time: 65.4 us; the launch traced here: 65.3 us
  Pallas kernels  65.1 us (100%)
    pallas_call x1, Pallas kernels, on_device(): pl.pallas_call(channelize, out_shape=[jax.ShapeDtypeStruct((2, 128, 4, 16...  59.2 us
    pallas_call x1, Pallas kernels, on_device(): pl.pallas_call(correlate, out_shape=jax.ShapeDtypeStruct((4, 2, 512, 512)...  5.88 us

profile of v4, /device:TPU:1, one launch (start us, length us, event | category | flops | bytes accessed | tf_op | source)
XLA Modules:
  0.0 65.3 jit_solution(4974482870553855543)
XLA Ops:
  0.0 59.2 %channelize.1 = (bf16[2,128,4,16,128]{4,3,2,1,0:T(8,128)(2,1)}, f32[2,2,512,512]{3,2,1,0:T(8,128)}) custom-call(bf16[64,35840]{1,0:T(8,128)(2,1)} %volt.1, f32[4,1024]{1,0:T(4,128)} %constant.4.clone.window, bf16[1024,1024]{1,0:T(8,128)(2,1)} %constant.5.clone.table), custom_call_target="tpu_custom_call" | custom-call | tf_op jit(solution)/shard_map/channelize/pallas_call | solution.py:311
  59.3 5.9 %correlate.1 = f32[4,2,512,512]{3,2,1,0:T(8,128)} custom-call(bf16[2,128,4,16,128]{4,3,2,1,0:T(8,128)(2,1)} %get-tuple-element.7.block, f32[2,2,512,512]{3,2,1,0:T(8,128)} %get-tuple-element.8.early), custom_call_target="tpu_custom_call" | custom-call | tf_op jit(solution)/shard_map/correlate/pallas_call | solution.py:341

commit v5 on v4

--- a/solution.py
+++ b/solution.py
@@ -139,7 +139,7 @@
         pltpu.make_async_copy(window, taps, row_sem.at[0]),
         pltpu.make_async_copy(table, whole, row_sem.at[1]),
     ]
-    for load in small[:1] + loads[:4] + small[1:] + loads[4:]:
+    for load in small[:1] + loads[:4]:
         load.start()
 
     def onward(at, step):
@@ -157,7 +157,7 @@
         return ys[dy] + upper[dz], xs[dx] + lower[dz]
 
     barrier = pltpu.get_barrier_semaphore()
-    for offset in ORDERS[0]:
+    for offset in ORDERS[1]:
         inp, tm = chip_at(offset)
         for side in range(2):
             if (offset, side) != ((0, 0, 0), 0):
@@ -208,6 +208,8 @@
     for h in range(2):
         for i in range(INPUTS // 16):
             loads[4 * h + i].wait()
+            if h == 0 and i == 0:
+                small[1].start()
 
             def filter_tile(j, carry, i=i, h=h):
                 at = pl.multiple_of(j * 128, 128)
@@ -226,6 +228,8 @@
 
             lax.fori_loop(0, FRAME // 128, filter_tile, 0)
         if h == 0:
+            for load in loads[4:]:
+                load.start()
             small[1].wait()
 
         for chunk in range(CHIPS // CHUNK):
@@ -281,7 +285,7 @@
         for c in range(2)
     ]
     moves = [pltpu.make_async_copy(early.at[c], passed.at[c], early_sem.at[c]) for c in range(2)]
-    for load in loads[0] + moves + loads[1]:
+    for load in moves + loads[0] + loads[1]:
         load.start()
     stores = []
     for h in range(2):

time: 65.4 us -> 64.9 us (level)
  no operation moved by 1% of the time
where the time goes in v5:
time: 64.9 us; the launch traced here: 64.7 us
  Pallas kernels  64.5 us (99%)
    pallas_call x1, Pallas kernels, on_device(): pl.pallas_call(channelize, out_shape=[jax.ShapeDtypeStruct((2, 128, 4, 16...  58.7 us
    pallas_call x1, Pallas kernels, on_device(): pl.pallas_call(correlate, out_shape=jax.ShapeDtypeStruct((4, 2, 512, 512)...  5.88 us

profile of v5, /device:TPU:1, one launch (start us, length us, event | category | flops | bytes accessed | tf_op | source)
XLA Modules:
  0.0 64.7 jit_solution(13009066239354776967)
XLA Ops:
  0.0 58.7 %channelize.1 = (bf16[2,128,4,16,128]{4,3,2,1,0:T(8,128)(2,1)}, f32[2,2,512,512]{3,2,1,0:T(8,128)}) custom-call(bf16[64,35840]{1,0:T(8,128)(2,1)} %volt.1, f32[4,1024]{1,0:T(4,128)} %constant.4.clone.window, bf16[1024,1024]{1,0:T(8,128)(2,1)} %constant.5.clone.table), custom_call_target="tpu_custom_call" | custom-call | tf_op jit(solution)/shard_map/channelize/pallas_call | solution.py:315
  58.7 5.9 %correlate.1 = f32[4,2,512,512]{3,2,1,0:T(8,128)} custom-call(bf16[2,128,4,16,128]{4,3,2,1,0:T(8,128)(2,1)} %get-tuple-element.7.block, f32[2,2,512,512]{3,2,1,0:T(8,128)} %get-tuple-element.8.early), custom_call_target="tpu_custom_call" | custom-call | tf_op jit(solution)/shard_map/correlate/pallas_call | solution.py:345

commit v6 on v5

--- a/solution.py
+++ b/solution.py
@@ -19,7 +19,7 @@
 PAIRS = 8
 CHIPS = 64
 UNIT = 16
-CHUNK = 16
+CHUNK = 8
 ROWS = CHUNK * UNIT
 PITCH = ROWS + 8
 TOTAL = 512

time: 64.9 us -> 66.3 us (1.022)
  Pallas kernels: 64.5 us -> 65.9 us
    pallas_call x1, Pallas kernels: 58.7 us -> 60.1 us  [on_device(): pl.pallas_call(channelize, out_shape=[jax.ShapeDtypeStruct((2, 128, 4, 16...]
where the time goes in v6:
time: 66.3 us; the launch traced here: 66.1 us
  Pallas kernels  65.9 us (99%)
    pallas_call x1, Pallas kernels, on_device(): pl.pallas_call(channelize, out_shape=[jax.ShapeDtypeStruct((2, 128, 4, 16...  60.1 us
    pallas_call x1, Pallas kernels, on_device(): pl.pallas_call(correlate, out_shape=jax.ShapeDtypeStruct((4, 2, 512, 512)...  5.88 us

profile of v6, /device:TPU:1, one launch (start us, length us, event | category | flops | bytes accessed | tf_op | source)
XLA Modules:
  0.0 66.1 jit_solution(245851779888416599)
XLA Ops:
  0.0 60.1 %channelize.1 = (bf16[2,128,4,16,128]{4,3,2,1,0:T(8,128)(2,1)}, f32[2,2,512,512]{3,2,1,0:T(8,128)}) custom-call(bf16[64,35840]{1,0:T(8,128)(2,1)} %volt.1, f32[4,1024]{1,0:T(4,128)} %constant.4.clone.window, bf16[1024,1024]{1,0:T(8,128)(2,1)} %constant.5.clone.table), custom_call_target="tpu_custom_call" | custom-call | tf_op jit(solution)/shard_map/channelize/pallas_call | solution.py:315
  60.1 5.9 %correlate.1 = f32[4,2,512,512]{3,2,1,0:T(8,128)} custom-call(bf16[2,128,4,16,128]{4,3,2,1,0:T(8,128)(2,1)} %get-tuple-element.7.block, f32[2,2,512,512]{3,2,1,0:T(8,128)} %get-tuple-element.8.early), custom_call_target="tpu_custom_call" | custom-call | tf_op jit(solution)/shard_map/correlate/pallas_call | solution.py:345
